TPU v7x, 256 devices: a whole 4x4x8 slice. The times are simulated.
256 devices in a mesh: section: 32 (over z, y_lo, core), dp: 8 (over x, y_hi).
Axes of the slice: x: 4, y: 4 (y_hi: 2, y_lo: 2; y = y_hi * 2 + y_lo), z: 8, core: 2. Of those that a mesh axis runs over, the one named last changes fastest.
Arguments:
- entry_codes: bfloat16 [4, 128, 12288], P(None, 'dp', 'section'), may hold values from -16 to 16
- loss_target: bfloat16 [4, 128, 12288], P(None, 'dp', 'section'), may hold values from -6 to 6
- fwd_inflow: bfloat16 [32, 128, 12288], P('section', 'dp'), may hold values from -16 to 16
- bwd_inflow: bfloat16 [32, 128, 12288], P('section', 'dp'), may hold values from -16 to 16
- act_cache: bfloat16 [32, 32, 16, 12288], P('section', 'dp'), may hold values from -6 to 6
- act_exps: int32 [32, 32, 16, 96], P('section', 'dp'), may hold values from -5 to -1
- grad_cache: bfloat16 [32, 32, 16, 12288], P('section', 'dp'), may hold values from -6 to 6
- grad_exps: int32 [32, 32, 16, 96], P('section', 'dp'), may hold values from -5 to -1
- fwd_rows: int32 [32, 32], P('section', 'dp'), may hold values from 0 to 3, as said below
- bwd_rows: int32 [32, 32], P('section', 'dp'), may hold values from 0 to 3, as said below
- norm_gain: bfloat16 [32, 12288], P('section'), may hold values from 0.5 to 2
- w_in: bfloat16 [32, 64, 12288], P('section'), may hold values from -0.0546875 to 0.0546875
- w_out: bfloat16 [32, 64, 12288], P('section'), may hold values from -0.75 to 0.75
Outputs:
- grad_w_in: bfloat16 [32, 64, 12288], P('section', None, 'dp')
- grad_w_out: bfloat16 [32, 64, 12288], P('section', None, 'dp')
- grad_gain: float32 [32, 12288], P('section', 'dp')
- fwd_outflow: bfloat16 [32, 128, 12288], P('section', 'dp')
- bwd_outflow: bfloat16 [32, 128, 12288], P('section', 'dp')
Inputs may be any that keep to these rules, and one draw needn't show every extreme that they name: `fwd_rows`: each aligned block of 4 entries (one section, one data replica) names every row 0 to 3 once. `bwd_rows`: each aligned block of 4 entries (one section, one data replica) names every row 0 to 3 once.
All inputs are finite; a program needn't handle non-finite values.
Results may differ from a plain program's by a relative error of at most 0.017.
Values may be sent and summed in bfloat16 or wider, within the bound.
A program may use at most 128 MiB of HBM per device.

v0:
```python
import jax
import jax.numpy as jnp
from jax import lax
from jax.sharding import PartitionSpec as P

code_limit = 16.0


def passed_along(x, axis, by):
    count = lax.axis_size(axis)
    pairs = [(i, i + by) for i in range(count) if 0 <= i + by < count]
    return lax.ppermute(x, axis, pairs)


def blocks(values, scale):
    shaped = values.reshape(values.shape[:-1] + (scale.shape[-1], 128))
    return (shaped * scale[..., None]).reshape(values.shape)


def decode(cached, scale, code):
    return (cached.astype(jnp.float32) + blocks(code.astype(jnp.float32), scale)).astype(
        jnp.bfloat16
    )


def encode(values, cached, inverse):
    moved = blocks(values - cached.astype(jnp.float32), inverse)
    return jnp.clip(moved, -code_limit, code_limit).astype(jnp.bfloat16)


def gelu_slope(preactivation):
    return (
        0.5 * (1.0 + jax.scipy.special.erf(preactivation * 0.7071067811865476))
        + preactivation * jnp.exp(-0.5 * preactivation * preactivation) * 0.3989422804014327
    )


def layer_pieces(layer_in, gain_vector, first_weight, second_weight):
    input_float = layer_in.astype(jnp.float32)
    inverse_root_mean = lax.rsqrt(
        jnp.mean(input_float * input_float, axis=-1, keepdims=True) + 1e-05
    )
    normalized_input = input_float * inverse_root_mean
    normalized_rows = (normalized_input * gain_vector[None, :]).astype(jnp.bfloat16)
    preactivation = jnp.einsum(
        "rd,hd->rh", normalized_rows, first_weight, preferred_element_type=jnp.float32
    )
    active_rows = jax.nn.gelu(preactivation, approximate=False).astype(jnp.bfloat16)
    layer_output = input_float + jnp.dot(
        active_rows, second_weight, preferred_element_type=jnp.float32
    )
    return (
        layer_output,
        inverse_root_mean,
        normalized_input,
        normalized_rows,
        preactivation,
        active_rows,
    )


def body(
    entry_codes,
    loss_target,
    fwd_inflow,
    bwd_inflow,
    act_cache,
    act_exps,
    grad_cache,
    grad_exps,
    fwd_rows,
    bwd_rows,
    norm_gain,
    w_in,
    w_out,
):
    sections = lax.axis_size("section")
    section = lax.axis_index("section")
    ticks = entry_codes.shape[0]
    first = section == 0
    last = section == sections - 1
    act_power = act_exps[0][fwd_rows[0]].astype(jnp.float32)
    acts = act_cache[0][fwd_rows[0]]
    act_scale = jnp.exp2(act_power)
    back_rows = act_cache[0][bwd_rows[0]]
    grad_power = grad_exps[0][bwd_rows[0]].astype(jnp.float32)
    grads = grad_cache[0][bwd_rows[0]]
    grad_scale = jnp.exp2(grad_power)
    next_acts, next_inv = passed_along(
        (acts[1:], jnp.exp2(-act_power[1:]).astype(jnp.bfloat16)), "section", -1
    )
    prev_grads, prev_inv = passed_along(
        (grads[1:], jnp.exp2(-grad_power[1:]).astype(jnp.bfloat16)), "section", 1
    )
    next_inv = next_inv.astype(jnp.float32)
    prev_inv = prev_inv.astype(jnp.float32)
    entries, targets = (
        lax.all_gather(entry_codes, "section", axis=2, tiled=True),
        lax.all_gather(loss_target, "section", axis=2, tiled=True),
    )
    gain_vector = norm_gain[0].astype(jnp.float32)
    first_weight = w_in[0]
    second_weight = w_out[0]
    fwd_recv = fwd_inflow[0]
    bwd_recv = bwd_inflow[0]
    width = first_weight.shape[1]
    sum_first = jnp.zeros((first_weight.shape[0], width), jnp.float32)
    sum_second = jnp.zeros((first_weight.shape[0], width), jnp.float32)
    gain_gradient_sum = jnp.zeros((width,), jnp.float32)
    fwd_last = fwd_recv
    bwd_last = bwd_recv
    for tick in range(ticks):
        code = jnp.where(first, entries[tick], fwd_recv)
        layer_in = decode(acts[tick], act_scale[tick], code)
        layer_output = layer_pieces(layer_in, gain_vector, first_weight, second_weight)[0]
        if tick < ticks - 1:
            fwd_recv = passed_along(
                encode(layer_output, next_acts[tick], next_inv[tick]), "section", 1
            )
        else:
            fwd_last = layer_output.astype(jnp.bfloat16)
        loss_grad = (layer_output - targets[tick].astype(jnp.float32)).astype(jnp.bfloat16)
        grad_in = jnp.where(last, loss_grad, decode(grads[tick], grad_scale[tick], bwd_recv))
        backward_input = jnp.where(last, layer_in, back_rows[tick])
        (
            unused_slot,
            inverse_root_mean,
            normalized_input,
            normalized_rows,
            preactivation,
            active_rows,
        ) = layer_pieces(backward_input, gain_vector, first_weight, second_weight)
        d_active = jnp.einsum(
            "rd,hd->rh", grad_in, second_weight, preferred_element_type=jnp.float32
        )
        d_pre = (d_active * gelu_slope(preactivation)).astype(jnp.bfloat16)
        norm_gradient = jnp.dot(d_pre, first_weight, preferred_element_type=jnp.float32)
        sum_first = sum_first + jnp.einsum(
            "rh,rd->hd", d_pre, normalized_rows, preferred_element_type=jnp.float32
        )
        sum_second = sum_second + jnp.einsum(
            "rh,rd->hd", active_rows, grad_in, preferred_element_type=jnp.float32
        )
        gain_gradient_sum = gain_gradient_sum + jnp.sum(norm_gradient * normalized_input, axis=0)
        scaled_rows = norm_gradient * gain_vector[None, :]
        input_gradient = grad_in.astype(jnp.float32) + inverse_root_mean * (
            scaled_rows
            - normalized_input * jnp.mean(scaled_rows * normalized_input, axis=-1, keepdims=True)
        )
        if tick < ticks - 1:
            bwd_recv = passed_along(
                encode(input_gradient, prev_grads[tick], prev_inv[tick]), "section", -1
            )
        else:
            bwd_last = input_gradient.astype(jnp.bfloat16)
    replicas = lax.axis_size("dp")
    factor = 1.0 / (ticks * replicas)
    total_first, total_second, total_gain = (
        lax.psum(sum_first.astype(jnp.bfloat16), "dp").astype(jnp.float32),
        lax.psum(sum_second.astype(jnp.bfloat16), "dp").astype(jnp.float32),
        lax.psum(gain_gradient_sum.astype(jnp.bfloat16), "dp").astype(jnp.float32),
    )
    share = width // replicas
    start = lax.axis_index("dp") * share
    total_first = lax.dynamic_slice_in_dim(total_first, start, share, 1)
    total_second = lax.dynamic_slice_in_dim(total_second, start, share, 1)
    total_gain = lax.dynamic_slice_in_dim(total_gain, start, share, 0)
    grad_w_in = (total_first * factor).astype(jnp.bfloat16)[None]
    grad_w_out = (total_second * factor).astype(jnp.bfloat16)[None]
    grad_gain = (total_gain * factor)[None]
    return (grad_w_in, grad_w_out, grad_gain, fwd_last[None], bwd_last[None])


def solution(mesh):
    return jax.shard_map(
        body,
        mesh=mesh,
        in_specs=(
            P(None, "dp", "section"),
            P(None, "dp", "section"),
            P("section", "dp", None),
            P("section", "dp", None),
            P("section", "dp", None, None),
            P("section", "dp", None, None),
            P("section", "dp", None, None),
            P("section", "dp", None, None),
            P("section", "dp"),
            P("section", "dp"),
            P("section", None),
            P("section", None, None),
            P("section", None, None),
        ),
        out_specs=(
            P("section", None, "dp"),
            P("section", None, "dp"),
            P("section", "dp"),
            P("section", "dp", None),
            P("section", "dp", None),
        ),
        check_vma=False,
    )
```

profile of v0, /device:TPU:33, one launch (start us, length us, event | category | flops | bytes accessed | tf_op | source)
XLA Modules:
  0.0 411.4 jit_solution(2083566129814114762)
XLA Ops:
  10.5 2.6 collective-permute-start
  13.7 2.5 collective-permute-start.1
  16.2 3.2 gather_fusion.2
  19.4 2.4 slice.202
  21.8 3.1 collective-permute-start.3
  25.5 1.9 collective-permute-start.4
  27.5 1.8 gather_fusion.4
  30.2 3.2 collective-permute-done.1
  33.5 8.0 %collective-permute-done.4 = bf16[3,16,96]{2,1,0:T(8,128)(2,1)S(1)} collective-permute-done((bf16[3,16,96]{2,1,0:T(8,128)(2,1)S(1)}, bf16[3,16,96]{2,1,0:T(8,128)(2,1)S(1)}, u32[]{:S(2)}, u32[]{:S(2)}) %collective-permute-start.4) | collective-permute-done | bytes 9248 | tf_op jit(solution)/shard_map/ppermute | solution.py:12
  41.5 39.6 %all-gather.3.cloned.1.call-done = bf16[4,16,12288]{2,1,0:T(8,128)(2,1)} async-done(((bf16[4,16,384]{2,1,0:T(8,128)(2,1)}), bf16[4,16,12288]{2,1,0:T(8,128)(2,1)}) %all-gather.3.cloned.1.call-update) | async-done | bytes 1572880 | tf_op jit(solution)/shard_map/all_gather | solution.py:98
  81.1 2.1 fusion.122
  83.2 3.0 fusion.89
  87.2 58.4 %all-gather.5.cloned.1.call-done = bf16[4,16,12288]{2,1,0:T(8,128)(2,1)} async-done(((bf16[4,16,384]{2,1,0:T(8,128)(2,1)}), bf16[4,16,12288]{2,1,0:T(8,128)(2,1)}) %all-gather.5.cloned.1.call-update) | async-done | bytes 1572880 | tf_op jit(solution)/shard_map/all_gather | solution.py:99
  146.8 4.3 %fusion.161 = (bf16[16,12288]{1,0:T(8,128)(2,1)}, f32[16,12288]{1,0:T(8,128)}) fusion(f32[2,8,96,128]{3,2,1,0:T(8,128)} %bitcast.442, bf16[4,16,12288]{2,1,0:T(8,128)(2,1)} %gather_fusion.2, bf16[4,16,12288]{2,1,0:T(8,128)(2,1)} %all-gather.5.cloned.1.call-done, bf16[1,16,12288]{2,1,0:T(8,128)(2,1)} %param.16, pred[]{:T(512)S(6)} %eq.6, ...), kind=kOutput, calls=%fused_computation.196 | convolution fusion | flops 53347328 | bytes 7127105 | tf_op jit(solution)/shard_map/dot_general | solution.py:49
  151.4 1.9 fusion.150
  153.3 3.3 collective-permute-start.2
  159.1 2.4 fusion.87
  161.5 2.3 fusion.337
  163.8 1.9 collective-permute-start.5
  165.7 2.3 fusion.169
  168.2 2.5 fusion.100
  172.9 4.0 fusion.144
  176.8 3.9 collective-permute-start.6
  180.8 1.6 fusion.28
  182.6 1.8 fusion.162
  186.3 2.5 fusion.98
  188.8 1.9 collective-permute-start.7
  190.8 2.3 convolution_add_fusion.5
  193.4 2.3 convolution_add_fusion.2
  196.0 2.7 fusion.111
  200.8 4.0 fusion.138
  204.7 3.8 collective-permute-start.8
  210.4 1.8 fusion.163
  214.0 2.5 fusion.109
  216.6 2.9 collective-permute-start.9
  219.5 2.3 convolution_add_fusion.4
  222.1 2.3 convolution_add_fusion.1
  224.7 2.7 fusion.119
  228.3 3.4 convolution_add_fusion.6
  231.7 1.9 convert_bitcast_fusion.2
  233.6 1.6 fusion.16
  235.6 1.9 fusion.164
  239.5 1.8 fusion.1
  241.9 1.8 fusion
  243.8 36.6 %psum.23 = bf16[12288]{0:T(1024)(128)(2,1)S(1)} all-reduce(bf16[12288]{0:T(1024)(128)(2,1)S(1)} %add_convert_fusion), channel_id=1, replica_groups=mesh['section'=32,'dp'=8] {'dp'}, use_global_device_ids=true, to_apply=%region_17.18 | all-reduce | flops 12288 | bytes 49152 | tf_op jit(solution)/shard_map/psum | solution.py:161
  282.1 119.4 %all-reduce.3.cloned.1.call-done = (bf16[64,12288]{1,0:T(8,128)(2,1)}, bf16[64,12288]{1,0:T(8,128)(2,1)}) async-done(((bf16[64,12288]{1,0:T(8,128)(2,1)}, bf16[64,12288]{1,0:T(8,128)(2,1)}), (bf16[64,12288]{1,0:T(8,128)(2,1)}, bf16[64,12288]{1,0:T(8,128)(2,1)})) %all-reduce.3.cloned.1.call-update) | async-done | bytes 3145744 | tf_op jit(solution)/shard_map/psum | solution.py:159
  401.5 1.6 fusion.193
  403.2 1.6 fusion.192
  (145 shorter events, 27.4 us)
Async XLA Ops:
  7.2 1.5 copy-start
  7.2 73.9 %all-gather.3.cloned.1.call-start = ((), (), s32[]{:S(2)}) async-start(), calls=%async_computation | async-start | bytes 1622016 | tf_op jit(solution)/shard_map/all_gather | solution.py:98
  7.9 137.7 %all-gather.5.cloned.1.call-start = ((), (), s32[]{:S(2)}) async-start(), calls=%async_computation.1 | async-start | bytes 1622016 | tf_op jit(solution)/shard_map/all_gather | solution.py:99
  9.3 71.8 %copy-start.4 = (bf16[4,16,12288]{2,1,0:T(8,128)(2,1)}, bf16[4,16,12288]{2,1,0:T(8,128)(2,1)S(1)}, u32[]{:S(2)}) copy-start(bf16[4,16,12288]{2,1,0:T(8,128)(2,1)S(1)} %gather_fusion) | copy-start | bytes 4718596
  9.3 3.8 copy-start.31
  10.5 140.6 %collective-permute-start = (bf16[3,16,12288]{2,1,0:T(8,128)(2,1)}, bf16[3,16,12288]{2,1,0:T(8,128)(2,1)}, u32[]{:S(2)}, u32[]{:S(2)}) collective-permute-start(bf16[3,16,12288]{2,1,0:T(8,128)(2,1)} %slice.195), channel_id=1, source_target_pairs={{8,0},{16,8},{24,16},{32,24},{40,32},{48,40},{56,48},{64,56},{72,6... | collective-permute-start | bytes 3538952 | tf_op jit(solution)/shard_map/ppermute | solution.py:12
  13.7 19.8 %collective-permute-start.1 = (bf16[3,16,96]{2,1,0:T(8,128)(2,1)S(1)}, bf16[3,16,96]{2,1,0:T(8,128)(2,1)S(1)}, u32[]{:S(2)}, u32[]{:S(2)}) collective-permute-start(bf16[3,16,96]{2,1,0:T(8,128)(2,1)S(1)} %fusion.205), channel_id=1, source_target_pairs={{8,0},{16,8},{24,16},{32,24},{40,32},{48,40},{56,48},{64,56},{72,6... | collective-permute-start | bytes 27656 | tf_op jit(solution)/shard_map/ppermute | solution.py:12
  19.4 5.5 %copy-start.32 = (s32[1,4,16,96]{3,2,1,0:T(8,128)S(1)}, s32[1,4,16,96]{3,2,1,0:T(8,128)}, u32[]{:S(2)}) copy-start(s32[1,4,16,96]{3,2,1,0:T(8,128)} %param.20) | copy-start | bytes 73732
  21.8 137.0 %collective-permute-start.3 = (bf16[3,16,12288]{2,1,0:T(8,128)(2,1)}, bf16[3,16,12288]{2,1,0:T(8,128)(2,1)}, u32[]{:S(2)}, u32[]{:S(2)}) collective-permute-start(bf16[3,16,12288]{2,1,0:T(8,128)(2,1)} %slice.202), channel_id=1, source_target_pairs={{0,8},{8,16},{16,24},{24,32},{32,40},{40,48},{48,56},{56,64},{64,7... | collective-permute-start | bytes 3538952 | tf_op jit(solution)/shard_map/ppermute | solution.py:12
  25.5 16.0 %collective-permute-start.4 = (bf16[3,16,96]{2,1,0:T(8,128)(2,1)S(1)}, bf16[3,16,96]{2,1,0:T(8,128)(2,1)S(1)}, u32[]{:S(2)}, u32[]{:S(2)}) collective-permute-start(bf16[3,16,96]{2,1,0:T(8,128)(2,1)S(1)} %fusion.202), channel_id=1, source_target_pairs={{0,8},{8,16},{16,24},{24,32},{32,40},{40,48},{48,56},{56,64},{64,7... | collective-permute-start | bytes 27656 | tf_op jit(solution)/shard_map/ppermute | solution.py:12
  27.4 374.1 %all-reduce.3.cloned.1.call-start = ((), (), s32[]{:S(2)}) async-start(), calls=%async_computation.2 | async-start | bytes 6291456 | tf_op jit(solution)/shard_map/psum | solution.py:159
  29.4 0.8 copy-start.30
  29.6 53.6 %copy-start.16 = (f32[16,96,128]{2,1,0:T(8,128)}, f32[16,96,128]{2,1,0:T(8,128)S(1)}, u32[]{:S(2)}) copy-start(f32[16,96,128]{2,1,0:T(8,128)S(1)} %mul.618) | copy-start | bytes 2359300
  81.1 2.1 copy-start.29
  83.2 63.6 %copy-start.2 = (bf16[1,64,12288]{2,1,0:T(8,128)(2,1)S(1)}, bf16[1,64,12288]{2,1,0:T(8,128)(2,1)}, u32[]{:S(2)}) copy-start(bf16[1,64,12288]{2,1,0:T(8,128)(2,1)} %param.24) | copy-start | bytes 4718596
  83.2 63.6 %copy-start.3 = (bf16[1,64,12288]{2,1,0:T(8,128)(2,1)S(1)}, bf16[1,64,12288]{2,1,0:T(8,128)(2,1)}, u32[]{:S(2)}) copy-start(bf16[1,64,12288]{2,1,0:T(8,128)(2,1)} %param.25) | copy-start | bytes 4718596
  86.2 0.8 copy-start.25
  151.1 5.5 %copy-start.15 = (bf16[4,16,12288]{2,1,0:T(8,128)(2,1)S(1)}, bf16[4,16,12288]{2,1,0:T(8,128)(2,1)}, u32[]{:S(2)}) copy-start(bf16[4,16,12288]{2,1,0:T(8,128)(2,1)} %gather_fusion.4) | copy-start | bytes 4718596
  151.1 5.5 %copy-start.26 = (bf16[1,16,12288]{2,1,0:T(8,128)(2,1)S(1)}, bf16[1,16,12288]{2,1,0:T(8,128)(2,1)}, u32[]{:S(2)}) copy-start(bf16[1,16,12288]{2,1,0:T(8,128)(2,1)} %fusion.122) | copy-start | bytes 1179652
  153.3 4.0 copy-start.21
  153.3 14.7 %collective-permute-start.2 = (bf16[16,12288]{1,0:T(8,128)(2,1)S(1)}, bf16[16,12288]{1,0:T(8,128)(2,1)S(1)}, u32[]{:S(2)}, u32[]{:S(2)}) collective-permute-start(bf16[16,12288]{1,0:T(8,128)(2,1)S(1)} %fusion.150), channel_id=1, source_target_pairs={{0,8},{8,16},{16,24},{24,32},{32,40},{40,48},{48,56},{56,64},{64,7... | collective-permute-start | bytes 1179656 | tf_op jit(solution)/shard_map/ppermute | solution.py:12
  157.2 1.0 copy-start.18
  163.8 18.6 %collective-permute-start.5 = (bf16[16,12288]{1,0:T(8,128)(2,1)}, bf16[16,12288]{1,0:T(8,128)(2,1)}, u32[]{:S(2)}, u32[]{:S(2)}) collective-permute-start(bf16[16,12288]{1,0:T(8,128)(2,1)} %fusion.87), channel_id=1, source_target_pairs={{8,0},{16,8},{24,16},{32,24},{40,32},{48,40},{56,48},{64,56},{72,6... | collective-permute-start | bytes 1179656 | tf_op jit(solution)/shard_map/ppermute | solution.py:12
  170.7 0.7 copy-start.23
  176.8 5.8 %copy-start.28 = (f32[16,12288]{1,0:T(8,128)S(1)}, f32[16,12288]{1,0:T(8,128)}, u32[]{:S(2)}) copy-start(f32[16,12288]{1,0:T(8,128)} %get-tuple-element.45) | copy-start | bytes 2359300
  176.8 18.9 %collective-permute-start.6 = (bf16[16,12288]{1,0:T(8,128)(2,1)}, bf16[16,12288]{1,0:T(8,128)(2,1)S(1)}, u32[]{:S(2)}, u32[]{:S(2)}) collective-permute-start(bf16[16,12288]{1,0:T(8,128)(2,1)} %get-tuple-element.44), channel_id=1, source_target_pairs={{0,8},{8,16},{16,24},{24,32},{32,40},{40,48},{48,56},{56,64},{64,7... | collective-permute-start | bytes 1179656 | tf_op jit(solution)/shard_map/ppermute | solution.py:12
  184.5 1.0 copy-start.14
  186.3 4.5 %copy-start.8 = (f32[64,12288]{1,0:T(8,128)S(1)}, f32[64,12288]{1,0:T(8,128)}, u32[]{:S(2)}) copy-start(f32[64,12288]{1,0:T(8,128)} %fusion.169) | copy-start | bytes 9437188
  188.8 21.2 %collective-permute-start.7 = (bf16[16,12288]{1,0:T(8,128)(2,1)}, bf16[16,12288]{1,0:T(8,128)(2,1)}, u32[]{:S(2)}, u32[]{:S(2)}) collective-permute-start(bf16[16,12288]{1,0:T(8,128)(2,1)} %fusion.98), channel_id=1, source_target_pairs={{8,0},{16,8},{24,16},{32,24},{40,32},{48,40},{56,48},{64,56},{72,6... | collective-permute-start | bytes 1179656 | tf_op jit(solution)/shard_map/ppermute | solution.py:12
  190.8 2.6 copy-start.5
  198.6 0.7 copy-start.22
  204.7 5.7 %copy-start.27 = (f32[16,12288]{1,0:T(8,128)S(1)}, f32[16,12288]{1,0:T(8,128)}, u32[]{:S(2)}) copy-start(f32[16,12288]{1,0:T(8,128)} %get-tuple-element.48) | copy-start | bytes 2359300
  204.7 19.7 %collective-permute-start.8 = (bf16[16,12288]{1,0:T(8,128)(2,1)}, bf16[16,12288]{1,0:T(8,128)(2,1)S(1)}, u32[]{:S(2)}, u32[]{:S(2)}) collective-permute-start(bf16[16,12288]{1,0:T(8,128)(2,1)} %get-tuple-element.47), channel_id=1, source_target_pairs={{0,8},{8,16},{16,24},{24,32},{32,40},{40,48},{48,56},{56,64},{64,7... | collective-permute-start | bytes 1179656 | tf_op jit(solution)/shard_map/ppermute | solution.py:12
  212.2 1.0 copy-start.13
  214.0 5.5 %copy-start.6 = (f32[64,12288]{1,0:T(8,128)S(1)}, f32[64,12288]{1,0:T(8,128)}, u32[]{:S(2)}) copy-start(f32[64,12288]{1,0:T(8,128)} %convolution_add_fusion.5) | copy-start | bytes 9437188
  216.6 18.7 %collective-permute-start.9 = (bf16[16,12288]{1,0:T(8,128)(2,1)}, bf16[16,12288]{1,0:T(8,128)(2,1)}, u32[]{:S(2)}, u32[]{:S(2)}) collective-permute-start(bf16[16,12288]{1,0:T(8,128)(2,1)} %fusion.109), channel_id=1, source_target_pairs={{8,0},{16,8},{24,16},{32,24},{40,32},{48,40},{56,48},{64,56},{72,6... | collective-permute-start | bytes 1179656 | tf_op jit(solution)/shard_map/ppermute | solution.py:12
  219.5 2.6 copy-start.7
  227.3 0.7 copy-start.24
  233.6 1.9 copy-start.17
  235.6 2.4 copy-start.11
  237.4 1.1 copy-start.19
  237.5 2.0 copy-start.10
  239.5 2.5 copy-start.9
  243.8 37.3 %copy-start.12 = (bf16[16,12288]{1,0:T(8,128)(2,1)S(1)}, bf16[16,12288]{1,0:T(8,128)(2,1)}, u32[]{:S(2)}) copy-start(bf16[16,12288]{1,0:T(8,128)(2,1)} %get-tuple-element.16) | copy-start | bytes 1179652
  243.8 37.3 %copy-start.20 = (bf16[16,12288]{1,0:T(8,128)(2,1)S(1)}, bf16[16,12288]{1,0:T(8,128)(2,1)}, u32[]{:S(2)}) copy-start(bf16[16,12288]{1,0:T(8,128)(2,1)} %copy-done.19) | copy-start | bytes 1179652
  243.8 161.0 %copy-start.1 = (bf16[1,4,16,12288]{3,2,1,0:T(8,128)(2,1)S(1)}, bf16[1,4,16,12288]{3,2,1,0:T(8,128)(2,1)}, u32[]{:S(2)}) copy-start(bf16[1,4,16,12288]{3,2,1,0:T(8,128)(2,1)} %param.17) | copy-start | bytes 4718596
Sparse Core Ops, SparseCore 0:
  9.8 71.2 all-gather.2
  82.9 62.6 all-gather.4
  243.9 157.5 all-reduce.2
where the time goes:
time: 416 us; the launch traced here: 411 us
  waiting for transfers between devices  229 us (55%)
  matrix products  42.7 us (10%)
  blocking collectives  36.6 us (9%)
  other arithmetic  35.8 us (9%)
  starting transfers between devices  27.9 us (7%)
  local copies, waits for them, and re-layouts  24.6 us (6%)
  between operations  14.3 us (3%)
    psum x1, waiting for transfers between devices, body(): lax.psum(sum_first.astype(jnp.bfloat16), 'dp').astype(jnp.float32)  119 us
    all_gather x1, waiting for transfers between devices, body(): lax.all_gather(loss_target, 'section', axis=2, tiled=True)  58.4 us
    all_gather x1, waiting for transfers between devices, body(): lax.all_gather(entry_codes, 'section', axis=2, tiled=True)  39.6 us
    psum x1, blocking collectives, body(): lax.psum(gain_gradient_sum.astype(jnp.bfloat16), 'dp').astype(jnp.float32)  36.6 us
    ppermute x10, starting transfers between devices, passed_along(): return lax.ppermute(x, axis, pairs)  27.8 us
    dot_general x4, matrix products, layer_pieces(): jnp.dot(active_rows, second_weight, preferred_element_type=jnp.float32)  15.6 us
    reduce_sum x8, other arithmetic, layer_pieces(): jnp.mean(input_float * input_float, axis=-1, keepdims=True) + 1e-05  11.7 us
    ppermute x10, waiting for transfers between devices, passed_along(): return lax.ppermute(x, axis, pairs)  11.3 us
  transfers between devices with their start and end apart: 13, of which 5 were waited for; matrix products, arithmetic and copies ran while one was open for 21% of the time, Pallas kernels for 0%

commit v1 on v0

v1 whole, which is shorter than its diff:
```python
import functools

import jax
import jax.numpy as jnp
from jax import lax
from jax.experimental import pallas as pl
from jax.experimental.pallas import tpu as pltpu
from jax.sharding import PartitionSpec as P

MESH = pl.DeviceIdType.MESH
ROWS = 16
TICKS = 4
F32 = jnp.float32
BF16 = jnp.bfloat16


def dot_last(a, b):
    return lax.dot_general(a, b, (((1,), (1,)), ((), ())), preferred_element_type=F32)


def dot_first(a, b):
    return lax.dot_general(a, b, (((0,), (0,)), ((), ())), preferred_element_type=F32)


def dot_plain(a, b):
    return lax.dot_general(a, b, (((1,), (0,)), ((), ())), preferred_element_type=F32)


def half_erf(u):
    return 0.5 * (1.0 + lax.erf(u * 0.7071067811865476))


def gelu(u):
    return u * half_erf(u)


def gelu_slope(u):
    return half_erf(u) + u * jnp.exp(-0.5 * u * u) * 0.3989422804014327


def kernel(
    sections,
    replicas,
    fwd_rows,
    bwd_rows,
    gain_ref,
    act_exps,
    grad_exps,
    entry_hbm,
    target_hbm,
    fwd_inflow,
    bwd_inflow,
    act_hbm,
    grad_hbm,
    w_in_hbm,
    w_out_hbm,
    gw_in_out,
    gw_out_out,
    ggain_out,
    fwd_out,
    bwd_out,
    act,
    grad,
    w_in,
    w_out,
    wg,
    fwd_code,
    bwd_code,
    entries,
    targets,
    lim_act,
    lim_grad,
    x_back,
    x_now,
    g_all,
    y_send,
    y_recv,
    d_send,
    d_recv,
    u_back,
    r_back,
    a_back,
    du_tick,
    factors,
    x_gather,
    g_gather,
    f_gather,
    p_send,
    p_recv,
    load_sem,
    entry_send,
    entry_recv,
    y_send_sem,
    y_recv_sem,
    d_send_sem,
    d_recv_sem,
    x_send_sem,
    x_recv_sem,
    g_send_sem,
    g_recv_sem,
    f_send_sem,
    f_recv_sem,
    p_send_sem,
    p_recv_sem,
    out_sem,
):
    width = w_in.shape[1]
    ring = replicas // 2
    cut = width // ring
    share = width // replicas
    piece = width // sections
    inv_width = 1.0 / width
    s = lax.axis_index("section")
    p = lax.axis_index("dp")
    px = p // 2
    py = p % 2
    first = s == 0
    last = s == sections - 1
    not_first = s > 0
    not_last = s < sections - 1
    mate = px * 2 + (1 - py)

    barrier = pltpu.get_barrier_semaphore()

    def greet(where):
        pl.semaphore_signal(barrier, inc=1, device_id=where, device_id_type=MESH)

    @pl.when(not_first)
    def _():
        greet({"section": s - 1})

    @pl.when(not_last)
    def _():
        greet({"section": s + 1})

    for k in range(1, ring):
        greet({"dp": lax.rem(px + k, ring) * 2 + py})
    greet({"dp": mate})

    @pl.when(first)
    def _():
        def tell(i, c):
            greet({"section": i})
            return c

        lax.fori_loop(1, sections, tell, 0)

    @pl.when(last)
    def _():
        def tell(i, c):
            greet({"section": i})
            return c

        lax.fori_loop(0, sections - 1, tell, 0)

    loads = [
        pltpu.make_async_copy(src, dst, load_sem.at[i])
        for i, (src, dst) in enumerate(
            [
                (act_hbm, act),
                (w_in_hbm, w_in),
                (fwd_inflow, fwd_code),
                (w_out_hbm, w_out),
                (grad_hbm, grad),
                (bwd_inflow, bwd_code),
                (act_hbm, x_back),
            ]
        )
    ]
    for load in loads[:6]:
        load.start()

    @pl.when(not_last)
    def _():
        loads[6].start()

    count = (
        jnp.where(not_first, 2, 0) + jnp.where(not_last, 2, 0) + (ring - 1) + 1
    )
    pl.semaphore_wait(barrier, count)

    mine = pl.ds(pl.multiple_of(s * piece, 128), piece)

    def entry_copy(which, t):
        src = (entry_hbm, target_hbm)[which]
        dst = (entries, targets)[which]
        return pltpu.make_async_remote_copy(
            src_ref=src.at[t],
            dst_ref=dst.at[t, :, mine],
            send_sem=entry_send.at[which, t],
            recv_sem=entry_recv.at[which, t],
            device_id={"section": (0, sections - 1)[which]},
            device_id_type=MESH,
        )

    def entry_local(which, t):
        src = (entry_hbm, target_hbm)[which]
        dst = (entries, targets)[which]
        return pltpu.make_async_copy(
            src.at[t], dst.at[t, :, mine], entry_recv.at[which, t]
        )

    def entry_wait(which, t):
        dst = (entries, targets)[which]
        pltpu.make_async_copy(dst.at[t], dst.at[t], entry_recv.at[which, t]).wait()

    for t in range(TICKS):
        for which, away, here in ((0, not_first, first), (1, not_last, last)):

            @pl.when(away)
            def _():
                entry_copy(which, t).start()

            @pl.when(here)
            def _():
                entry_local(which, t).start()

    def columns(j):
        return pl.ds(pl.multiple_of(j * cut, 128), cut)

    def spread(src, dst, send_sem, recv_sem, slot, j):
        @pl.when(j != px)
        def _():
            pltpu.make_async_remote_copy(
                src_ref=src.at[slot, :, columns(j)],
                dst_ref=dst.at[px, slot],
                send_sem=send_sem.at[slot, j],
                recv_sem=recv_sem.at[px, slot],
                device_id={"dp": j * 2 + py},
                device_id_type=MESH,
            ).start()

        @pl.when(j == px)
        def _():
            pltpu.make_async_copy(
                src.at[slot, :, columns(j)], dst.at[px, slot], recv_sem.at[px, slot]
            ).start()

    def spread_wait(src, dst, send_sem, recv_sem):
        def one(i, c):
            k, slot = i // TICKS, i % TICKS

            @pl.when(k != px)
            def _():
                copy = pltpu.make_async_remote_copy(
                    src_ref=src.at[slot, :, columns(k)],
                    dst_ref=dst.at[k, slot],
                    send_sem=send_sem.at[slot, k],
                    recv_sem=recv_sem.at[k, slot],
                    device_id={"dp": k * 2 + py},
                    device_id_type=MESH,
                )
                copy.wait_recv()
                copy.wait_send()

            @pl.when(k == px)
            def _():
                pltpu.make_async_copy(
                    src.at[slot, :, columns(k)], dst.at[k, slot], recv_sem.at[k, slot]
                ).wait()

            return c

        lax.fori_loop(0, ring * TICKS, one, 0)

    def x_spread(slot, j):
        spread(x_back, x_gather, x_send_sem, x_recv_sem, slot, j)

    def g_spread(slot, j):
        spread(g_all, g_gather, g_send_sem, g_recv_sem, slot, j)

    @pl.when(not_last)
    def _():
        loads[6].wait()
        for slot in range(TICKS):
            for k in range(ring):
                x_spread(slot, lax.rem(px + k, ring))

    blocks = act_exps.shape[-1]
    group = min(8, blocks)
    wide = group * 128
    powers = jnp.concatenate(
        [
            act_exps[...].reshape(TICKS * ROWS, blocks),
            grad_exps[...].reshape(TICKS * ROWS, blocks),
        ],
        axis=0,
    ).astype(F32)
    scales = jnp.exp2(powers + 4.0).astype(BF16)

    def expand(j, c):
        at = pl.ds(pl.multiple_of(j * wide, 128), wide)
        row = lax.broadcasted_iota(jnp.int32, (blocks, wide), 0)
        col = lax.broadcasted_iota(jnp.int32, (blocks, wide), 1)
        pick = jnp.where(row == j * group + col // 128, 1.0, 0.0).astype(BF16)
        both = dot_plain(scales, pick).astype(BF16)
        lim_act[:, :, at] = both[: TICKS * ROWS].reshape(TICKS, ROWS, wide)
        lim_grad[:, :, at] = both[TICKS * ROWS :].reshape(TICKS, ROWS, wide)
        return c

    lax.fori_loop(0, blocks // group, expand, 0)

    loads[1].wait()

    def fold(j, c):
        wg[:, columns(j)] = (
            w_in[:, columns(j)].astype(F32) * gain_ref[:, columns(j)].astype(F32)
        ).astype(BF16)
        return c

    lax.fori_loop(0, ring, fold, 0)
    loads[0].wait()
    loads[2].wait()
    loads[3].wait()

    def y_copy(t, j):
        return pltpu.make_async_remote_copy(
            src_ref=y_send.at[t, :, columns(j)],
            dst_ref=y_recv.at[t, :, columns(j)],
            send_sem=y_send_sem.at[t, j],
            recv_sem=y_recv_sem.at[t, j],
            device_id={"section": s + 1},
            device_id_type=MESH,
        )

    def d_copy(t, j):
        return pltpu.make_async_remote_copy(
            src_ref=d_send.at[t, :, columns(j)],
            dst_ref=d_recv.at[t, :, columns(j)],
            send_sem=d_send_sem.at[t, j],
            recv_sem=d_recv_sem.at[t, j],
            device_id={"section": s - 1},
            device_id_type=MESH,
        )

    def scaled(cache, limit, code):
        return (
            cache.astype(F32) + limit.astype(F32) * 0.0625 * code.astype(F32)
        ).astype(BF16)

    def clipped(cache, limit, value):
        cache, limit, value = cache.astype(F32), limit.astype(F32), value.astype(F32)
        return jnp.minimum(jnp.maximum(value, cache - limit), cache + limit).astype(BF16)

    def forward(t):
        row = fwd_rows[0, t]

        @pl.when(first)
        def _():
            entry_wait(0, t)

        def take(j, c):
            total, u = c
            at = columns(j)
            cache, limit = act[row, :, at], lim_act[row, :, at]
            if t == 0:

                @pl.when(first)
                def _():
                    x_now[:, at] = scaled(cache, limit, entries[t, :, at])

                @pl.when(not_first)
                def _():
                    x_now[:, at] = scaled(cache, limit, fwd_code[:, at])

            else:

                @pl.when(first)
                def _():
                    x_now[:, at] = scaled(cache, limit, entries[t, :, at])

                @pl.when(not_first)
                def _():
                    y_copy(t - 1, j).wait_recv()
                    x_now[:, at] = clipped(cache, limit, y_recv[t - 1, :, at])

            x = x_now[:, at]
            xf = x.astype(F32)
            total = total + jnp.sum(xf * xf, axis=1, keepdims=True)
            u = u + dot_last(x, wg[:, at])

            @pl.when(last)
            def _():
                x_back[t, :, at] = x
                x_spread(t, j)

            return total, u

        total, u = lax.fori_loop(
            0,
            ring,
            take,
            (jnp.zeros((ROWS, 1), F32), jnp.zeros((ROWS, w_in.shape[0]), F32)),
        )
        r = lax.rsqrt(total * inv_width + 1e-05)
        u = u * r
        a = gelu(u).astype(BF16)

        @pl.when(last)
        def _():
            u_back[t] = u
            r_back[t] = jnp.broadcast_to(r, (ROWS, 128))
            a_back[t] = a
            entry_wait(1, t)

        def give(j, c):
            at = columns(j)
            y = x_now[:, at].astype(F32) + dot_plain(a, w_out[:, at])
            y_send[t, :, at] = y.astype(BF16)
            if t < TICKS - 1:

                @pl.when(not_last)
                def _():
                    y_copy(t, j).start()

            @pl.when(last)
            def _():
                g_all[t, :, at] = (y - targets[t, :, at].astype(F32)).astype(BF16)

            return c

        lax.fori_loop(0, ring, give, 0)
        if t == TICKS - 1:
            pltpu.make_async_copy(y_send.at[t], fwd_out, out_sem.at[0]).start()

    def prepare_backward():
        def take(j, c):
            total, u = c
            at = columns(j)
            x = x_back[:, :, at].reshape(TICKS * ROWS, cut)
            xf = x.astype(F32)
            return (
                total + jnp.sum(xf * xf, axis=1, keepdims=True),
                u + dot_last(x, wg[:, at]),
            )

        total, u = lax.fori_loop(
            0,
            ring,
            take,
            (
                jnp.zeros((TICKS * ROWS, 1), F32),
                jnp.zeros((TICKS * ROWS, w_in.shape[0]), F32),
            ),
        )
        r = lax.rsqrt(total * inv_width + 1e-05)
        u = u * r
        u_back[...] = u.reshape(u_back.shape)
        r_back[...] = jnp.broadcast_to(r, (TICKS * ROWS, 128)).reshape(r_back.shape)
        a_back[...] = gelu(u).astype(BF16).reshape(a_back.shape)

    def backward(t):
        row = bwd_rows[0, t]
        used = jnp.where(last, t, row)

        def take(j, c):
            at = columns(j)

            @pl.when(not_last)
            def _():
                cache, limit = grad[row, :, at], lim_grad[row, :, at]
                if t == 0:
                    g_all[t, :, at] = scaled(cache, limit, bwd_code[:, at])
                else:
                    d_copy(t - 1, j).wait_recv()
                    g_all[t, :, at] = clipped(cache, limit, d_recv[t - 1, :, at])

            g_spread(t, j)
            return c + dot_last(g_all[t, :, at], w_out[:, at])

        d_active = lax.fori_loop(
            0, ring, take, jnp.zeros((ROWS, w_in.shape[0]), F32)
        )
        u = u_back[used]
        r = r_back[used][:, :1]
        du = d_active * gelu_slope(u)
        shift = r * r * (jnp.sum(du * u, axis=1, keepdims=True) * inv_width)
        du_tick[t] = (du * r).astype(BF16)
        factors[1, t] = a_back[used]
        du = du.astype(BF16)

        def give(j, c):
            at = columns(j)
            dx = (
                g_all[t, :, at].astype(F32)
                + r * dot_plain(du, wg[:, at])
                - x_back[used, :, at].astype(F32) * shift
            )
            d_send[t, :, at] = dx.astype(BF16)
            if t < TICKS - 1:

                @pl.when(not_first)
                def _():
                    d_copy(t, j).start()

            return c

        lax.fori_loop(0, ring, give, 0)
        if t == TICKS - 1:
            pltpu.make_async_copy(d_send.at[t], bwd_out, out_sem.at[1]).start()

    def factor_copy(to, frm):
        return pltpu.make_async_remote_copy(
            src_ref=factors,
            dst_ref=f_gather.at[frm],
            send_sem=f_send_sem.at[to],
            recv_sem=f_recv_sem.at[frm],
            device_id={"dp": to * 2 + py},
            device_id_type=MESH,
        )

    forward(0)
    loads[4].wait()
    loads[5].wait()

    @pl.when(not_last)
    def _():
        prepare_backward()

    backward(0)
    for t in range(1, TICKS):
        forward(t)
        backward(t)

    used = [jnp.where(last, t, bwd_rows[0, t]) for t in range(TICKS)]
    for q in range(TICKS):
        at = 0
        for t in range(1, TICKS):
            at = jnp.where(used[t] == q, t, at)
        factors[0, q] = du_tick[at]
    for k in range(1, ring):
        factor_copy(lax.rem(px + k, ring), px).start()
    own = pltpu.make_async_copy(factors, f_gather.at[px], f_recv_sem.at[px])
    own.start()
    spread_wait(x_back, x_gather, x_send_sem, x_recv_sem)
    spread_wait(g_all, g_gather, g_send_sem, g_recv_sem)
    own.wait()
    for k in range(1, ring):
        other = lax.rem(px + k, ring)
        factor_copy(other, other).wait()

    rows = ring * TICKS * ROWS
    win = w_in.shape[0]
    du_rows = f_gather[:, 0].reshape(rows, win)
    a_rows = f_gather[:, 1].reshape(rows, win)

    def products(half):
        at = pl.ds(pl.multiple_of(half * share, 128), share)
        return (
            dot_first(du_rows, x_gather[:, :, :, at].reshape(rows, share)),
            dot_first(a_rows, g_gather[:, :, :, at].reshape(rows, share)),
        )

    in_part, out_part = products(1 - py)
    p_send[0] = in_part.astype(BF16)
    p_send[1] = out_part.astype(BF16)
    swap = pltpu.make_async_remote_copy(
        src_ref=p_send,
        dst_ref=p_recv,
        send_sem=p_send_sem,
        recv_sem=p_recv_sem,
        device_id={"dp": mate},
        device_id_type=MESH,
    )
    swap.start()
    in_part, out_part = products(py)
    swap.wait()
    in_part = in_part + p_recv[0].astype(F32)
    out_part = out_part + p_recv[1].astype(F32)
    factor = 1.0 / (TICKS * replicas)
    at = pl.ds(pl.multiple_of(p * share, 128), share)
    gw_in_out[...] = (in_part * (gain_ref[:, at].astype(F32) * factor)).astype(BF16)
    gw_out_out[...] = (out_part * factor).astype(BF16)
    ggain_out[...] = (
        jnp.sum(in_part * w_in[:, at].astype(F32), axis=0, keepdims=True) * factor
    )

    for t in range(TICKS):

        @pl.when(not_first)
        def _():
            entry_copy(0, t).wait_send()

        @pl.when(not_last)
        def _():
            entry_copy(1, t).wait_send()

    for t in range(TICKS - 1):
        for j in range(ring):

            @pl.when(not_last)
            def _():
                y_copy(t, j).wait_send()

            @pl.when(not_first)
            def _():
                d_copy(t, j).wait_send()

    pltpu.make_async_copy(y_send.at[TICKS - 1], fwd_out, out_sem.at[0]).wait()
    pltpu.make_async_copy(d_send.at[TICKS - 1], bwd_out, out_sem.at[1]).wait()


def solution(mesh):
    sections = mesh.shape["section"]
    replicas = mesh.shape["dp"]

    def body(
        entry_codes,
        loss_target,
        fwd_inflow,
        bwd_inflow,
        act_cache,
        act_exps,
        grad_cache,
        grad_exps,
        fwd_rows,
        bwd_rows,
        norm_gain,
        w_in,
        w_out,
    ):
        win, width = w_in.shape[1:]
        ring = replicas // 2
        cut = width // ring
        share = width // replicas
        blocks = act_exps.shape[-1]
        full = (ROWS, width)
        dma = pltpu.SemaphoreType.DMA
        hbm = pl.BlockSpec(memory_space=pl.ANY)
        vmem = pl.BlockSpec(memory_space=pltpu.VMEM)
        smem = pl.BlockSpec(memory_space=pltpu.SMEM)
        outs = pl.pallas_call(
            functools.partial(kernel, sections, replicas),
            out_shape=(
                jax.ShapeDtypeStruct((win, share), BF16),
                jax.ShapeDtypeStruct((win, share), BF16),
                jax.ShapeDtypeStruct((1, share), F32),
                jax.ShapeDtypeStruct(full, BF16),
                jax.ShapeDtypeStruct(full, BF16),
            ),
            in_specs=[smem, smem, vmem, vmem, vmem] + [hbm] * 8,
            out_specs=(vmem, vmem, vmem, hbm, hbm),
            scratch_shapes=[
                pltpu.VMEM((TICKS,) + full, BF16),
                pltpu.VMEM((TICKS,) + full, BF16),
                pltpu.VMEM((win, width), BF16),
                pltpu.VMEM((win, width), BF16),
                pltpu.VMEM((win, width), BF16),
                pltpu.VMEM(full, BF16),
                pltpu.VMEM(full, BF16),
                pltpu.VMEM((TICKS,) + full, BF16),
                pltpu.VMEM((TICKS,) + full, BF16),
                pltpu.VMEM((TICKS,) + full, BF16),
                pltpu.VMEM((TICKS,) + full, BF16),
                pltpu.VMEM((TICKS,) + full, BF16),
                pltpu.VMEM(full, BF16),
                pltpu.VMEM((TICKS,) + full, BF16),
                pltpu.VMEM((TICKS,) + full, BF16),
                pltpu.VMEM((TICKS - 1,) + full, BF16),
                pltpu.VMEM((TICKS,) + full, BF16),
                pltpu.VMEM((TICKS - 1,) + full, BF16),
                pltpu.VMEM((TICKS, ROWS, win), F32),
                pltpu.VMEM((TICKS, ROWS, 128), F32),
                pltpu.VMEM((TICKS, ROWS, win), BF16),
                pltpu.VMEM((TICKS, ROWS, win), BF16),
                pltpu.VMEM((2, TICKS, ROWS, win), BF16),
                pltpu.VMEM((ring, TICKS, ROWS, cut), BF16),
                pltpu.VMEM((ring, TICKS, ROWS, cut), BF16),
                pltpu.VMEM((ring, 2, TICKS, ROWS, win), BF16),
                pltpu.VMEM((2, win, share), BF16),
                pltpu.VMEM((2, win, share), BF16),
                dma((7,)),
                dma((2, TICKS)),
                dma((2, TICKS)),
                dma((TICKS - 1, ring)),
                dma((TICKS - 1, ring)),
                dma((TICKS - 1, ring)),
                dma((TICKS - 1, ring)),
                dma((TICKS, ring)),
                dma((ring, TICKS)),
                dma((TICKS, ring)),
                dma((ring, TICKS)),
                dma((ring,)),
                dma((ring,)),
                dma,
                dma,
                dma((2,)),
            ],
            compiler_params=pltpu.CompilerParams(
                collective_id=0,
                has_side_effects=True,
                vmem_limit_bytes=48 * 1024 * 1024,
            ),
        )(
            fwd_rows,
            bwd_rows,
            norm_gain,
            act_exps[0],
            grad_exps[0],
            entry_codes,
            loss_target,
            fwd_inflow[0],
            bwd_inflow[0],
            act_cache[0],
            grad_cache[0],
            w_in[0],
            w_out[0],
        )
        gw_in, gw_out, ggain, fwd_last, bwd_last = outs
        return gw_in[None], gw_out[None], ggain, fwd_last[None], bwd_last[None]

    return jax.shard_map(
        body,
        mesh=mesh,
        in_specs=(
            P(None, "dp", "section"),
            P(None, "dp", "section"),
            P("section", "dp", None),
            P("section", "dp", None),
            P("section", "dp", None, None),
            P("section", "dp", None, None),
            P("section", "dp", None, None),
            P("section", "dp", None, None),
            P("section", "dp"),
            P("section", "dp"),
            P("section", None),
            P("section", None, None),
            P("section", None, None),
        ),
        out_specs=(
            P("section", None, "dp"),
            P("section", None, "dp"),
            P("section", "dp"),
            P("section", "dp", None),
            P("section", "dp", None),
        ),
        check_vma=False,
    )
```

time: 416 us -> 75.5 us (0.18)
  the two profiles are of different devices: /device:TPU:33 before, /device:TPU:1 now
where the time goes in v1:
time: 75.5 us; the launch traced here: 75 us
  Pallas kernels  60.9 us (81%)
  local copies, waits for them, and re-layouts  13.5 us (18%)
    pallas_call x1, Pallas kernels, body(): pl.pallas_call(functools.partial(kernel, sections, replicas), out_shape=(...  60.9 us
    unnamed x27, local copies, waits for them, and re-layouts  13.5 us

profile of v1, /device:TPU:1, one launch (start us, length us, event | category | flops | bytes accessed | tf_op | source)
XLA Modules:
  0.0 75.0 jit_solution(14167381876177648524)
XLA Ops:
  0.6 0.0 copy-start
  0.6 1.4 %copy-done = bf16[1,4,16,12288]{3,2,1,0:T(8,128)(2,1)S(1)} copy-done((bf16[1,4,16,12288]{3,2,1,0:T(8,128)(2,1)S(1)}, bf16[1,4,16,12288]{3,2,1,0:T(8,128)(2,1)}, u32[]{:S(2)}) %copy-start) | copy-done | bytes 1572888
  2.0 0.0 copy-start.1
  2.0 1.4 %copy-done.1 = bf16[1,4,16,12288]{3,2,1,0:T(8,128)(2,1)S(1)} copy-done((bf16[1,4,16,12288]{3,2,1,0:T(8,128)(2,1)S(1)}, bf16[1,4,16,12288]{3,2,1,0:T(8,128)(2,1)}, u32[]{:S(2)}) %copy-start.1) | copy-done | bytes 1572888
  3.5 0.0 copy-start.2
  3.5 1.0 %copy-done.2 = bf16[1,16,12288]{2,1,0:T(8,128)(2,1)S(1)} copy-done((bf16[1,16,12288]{2,1,0:T(8,128)(2,1)S(1)}, bf16[1,16,12288]{2,1,0:T(8,128)(2,1)}, u32[]{:S(2)}) %copy-start.2) | copy-done | bytes 393240
  4.5 0.0 copy-start.3
  4.5 1.0 %copy-done.3 = bf16[1,16,12288]{2,1,0:T(8,128)(2,1)S(1)} copy-done((bf16[1,16,12288]{2,1,0:T(8,128)(2,1)S(1)}, bf16[1,16,12288]{2,1,0:T(8,128)(2,1)}, u32[]{:S(2)}) %copy-start.3) | copy-done | bytes 393240
  5.4 0.0 copy-start.4
  5.4 0.8 %copy-done.4 = bf16[1,12288]{1,0:T(2,128)(2,1)S(1)} copy-done((bf16[1,12288]{1,0:T(2,128)(2,1)S(1)}, bf16[1,12288]{1,0:T(2,128)(2,1)}, u32[]{:S(2)}) %copy-start.4) | copy-done | bytes 24600
  6.2 0.0 copy-start.5
  6.2 0.8 %copy-done.5 = bf16[4,16,384]{2,1,0:T(8,128)(2,1)S(1)} copy-done((bf16[4,16,384]{2,1,0:T(8,128)(2,1)S(1)}, bf16[4,16,384]{2,1,0:T(8,128)(2,1)}, u32[]{:S(2)}) %copy-start.5) | copy-done | bytes 49176
  7.0 0.0 copy-start.6
  7.0 0.8 %copy-done.6 = bf16[4,16,384]{2,1,0:T(8,128)(2,1)S(1)} copy-done((bf16[4,16,384]{2,1,0:T(8,128)(2,1)S(1)}, bf16[4,16,384]{2,1,0:T(8,128)(2,1)}, u32[]{:S(2)}) %copy-start.6) | copy-done | bytes 49176
  7.8 0.0 copy-start.7
  7.8 0.8 %copy-done.7 = s32[1,4,16,96]{3,2,1,0:T(8,128)S(1)} copy-done((s32[1,4,16,96]{3,2,1,0:T(8,128)S(1)}, s32[1,4,16,96]{3,2,1,0:T(8,128)}, u32[]{:S(2)}) %copy-start.7) | copy-done | bytes 24600
  8.6 0.0 copy-start.8
  8.6 0.8 %copy-done.8 = s32[1,4,16,96]{3,2,1,0:T(8,128)S(1)} copy-done((s32[1,4,16,96]{3,2,1,0:T(8,128)S(1)}, s32[1,4,16,96]{3,2,1,0:T(8,128)}, u32[]{:S(2)}) %copy-start.8) | copy-done | bytes 24600
  9.4 0.0 copy-start.9
  9.4 0.7 copy-done.9
  10.0 0.0 copy-start.10
  10.0 0.7 copy-done.10
  10.7 60.9 %shard_map.164 = (bf16[64,1536]{1,0:T(8,128)(2,1)S(1)}, bf16[64,1536]{1,0:T(8,128)(2,1)S(1)}, f32[1,1536]{1,0:T(1,128)S(1)}, bf16[16,12288]{1,0:T(8,128)(2,1)S(1)}, bf16[16,12288]{1,0:T(8,128)(2,1)S(1)}) custom-call(s32[1,4]{1,0:T(1,128)S(1)} %copy-done.9, s32[1,4]{1,0:T(1,128)S(1)} %copy-done.10, bf16[1,12288]{1,0:T(2,128)(2,1)S(1)} %copy-done.4, ...), custom_call_target="tpu_custom_call" | custom-call | tf_op jit(solution)/shard_map/pallas_call | solution.py:632
  71.6 0.7 copy.23
  72.2 0.7 copy.24
  72.9 0.6 copy.25
  73.5 0.7 copy.26
  74.3 0.7 copy.27
Async XLA Ops:
  0.6 1.4 %copy-start = (bf16[1,4,16,12288]{3,2,1,0:T(8,128)(2,1)S(1)}, bf16[1,4,16,12288]{3,2,1,0:T(8,128)(2,1)}, u32[]{:S(2)}) copy-start(bf16[1,4,16,12288]{3,2,1,0:T(8,128)(2,1)} %param.17) | copy-start | bytes 4718596
  2.0 1.4 %copy-start.1 = (bf16[1,4,16,12288]{3,2,1,0:T(8,128)(2,1)S(1)}, bf16[1,4,16,12288]{3,2,1,0:T(8,128)(2,1)}, u32[]{:S(2)}) copy-start(bf16[1,4,16,12288]{3,2,1,0:T(8,128)(2,1)} %param.19) | copy-start | bytes 4718596
  3.5 1.0 %copy-start.2 = (bf16[1,16,12288]{2,1,0:T(8,128)(2,1)S(1)}, bf16[1,16,12288]{2,1,0:T(8,128)(2,1)}, u32[]{:S(2)}) copy-start(bf16[1,16,12288]{2,1,0:T(8,128)(2,1)} %param.15) | copy-start | bytes 1179652
  4.5 1.0 %copy-start.3 = (bf16[1,16,12288]{2,1,0:T(8,128)(2,1)S(1)}, bf16[1,16,12288]{2,1,0:T(8,128)(2,1)}, u32[]{:S(2)}) copy-start(bf16[1,16,12288]{2,1,0:T(8,128)(2,1)} %param.16) | copy-start | bytes 1179652
  5.4 0.8 %copy-start.4 = (bf16[1,12288]{1,0:T(2,128)(2,1)S(1)}, bf16[1,12288]{1,0:T(2,128)(2,1)}, u32[]{:S(2)}) copy-start(bf16[1,12288]{1,0:T(2,128)(2,1)} %gain_ref.1) | copy-start | bytes 73732
  6.2 0.8 %copy-start.5 = (bf16[4,16,384]{2,1,0:T(8,128)(2,1)S(1)}, bf16[4,16,384]{2,1,0:T(8,128)(2,1)}, u32[]{:S(2)}) copy-start(bf16[4,16,384]{2,1,0:T(8,128)(2,1)} %entry_hbm.1) | copy-start | bytes 147460
  7.0 0.8 %copy-start.6 = (bf16[4,16,384]{2,1,0:T(8,128)(2,1)S(1)}, bf16[4,16,384]{2,1,0:T(8,128)(2,1)}, u32[]{:S(2)}) copy-start(bf16[4,16,384]{2,1,0:T(8,128)(2,1)} %target_hbm.1) | copy-start | bytes 147460
  7.8 0.8 %copy-start.7 = (s32[1,4,16,96]{3,2,1,0:T(8,128)S(1)}, s32[1,4,16,96]{3,2,1,0:T(8,128)}, u32[]{:S(2)}) copy-start(s32[1,4,16,96]{3,2,1,0:T(8,128)} %param.18) | copy-start | bytes 73732
  8.6 0.8 %copy-start.8 = (s32[1,4,16,96]{3,2,1,0:T(8,128)S(1)}, s32[1,4,16,96]{3,2,1,0:T(8,128)}, u32[]{:S(2)}) copy-start(s32[1,4,16,96]{3,2,1,0:T(8,128)} %param.20) | copy-start | bytes 73732
  9.4 0.7 copy-start.9
  10.0 0.7 copy-start.10
